TPU v7x, 32 devices: a whole 2x2x4 slice. The times are simulated.
32 devices in a mesh: sec: 2 (over y), col: 4 (over z), row: 4 (over x, core).
Axes of the slice: x: 2, y: 2, z: 4, core: 2. Of those that a mesh axis runs over, the one named last changes fastest.
Arguments:
- ancestor: float32 [16384, 16384], P('row', ('sec', 'col')), may hold values from -0.3 to 0.3
- panel: float32 [2, 8192, 2048], P('sec', 'row', 'col'), may hold values from -1.5 to 1.5
- diag_inverse: float32 [2, 2048, 2048], P('sec', 'col', 'row'), may hold values from -12 to 12
- frontier: int32 [2, 16, 4], replicated, may hold values from 0 to 7, as said below
- counts: int32 [2, 16], replicated, may hold values from 1 to 4
- pattern: int32 [2, 64, 64], replicated, may hold values 0 or 1
Outputs:
- cross_block: float32 [2, 2048, 8192], P('sec', 'col', 'row')
- inverse: float32 [2, 2048, 2048], P('sec', 'col', 'row')
Inputs may be any that keep to these rules, and one draw needn't show every extreme that they name: The 4 offsets of one child and group are distinct; slot j of group g is ancestor tile 8 * g + frontier[c, g, j]. Slots j >= counts[c, g] of group g are padding for child c.
All inputs are finite; a program needn't handle non-finite values.
Results may differ from a plain program's by a relative error of at most 0.0001.
Values sent between devices are 32-bit elements; how exact they have to be, the bound alone decides.
A program may use at most 256 MiB of HBM per device.

v0:
```python
import jax
import jax.numpy as jnp
from jax import lax
from jax.sharding import PartitionSpec as P

TILE = 128
GROUP = 8
SLOTS = 4


def swapped(value, axis, distance):
    mask = 2**distance
    pairs = [(source, source ^ mask) for source in range(lax.axis_size(axis))]
    return lax.ppermute(value, axis, pairs)


def from_root(value, axis, source):
    kept = jnp.where(lax.axis_index(axis) == source, value, 0).astype(value.dtype)
    return lax.psum(kept, axis)


def pick_tiles(
    ancestor, frontier, counts, pattern, child_id, row_start, block_start, row_groups, block_groups
):
    offsets = lax.dynamic_index_in_dim(frontier, child_id, 0, keepdims=False)
    sizes_live = lax.dynamic_index_in_dim(counts, child_id, 0, keepdims=False)
    pattern_child = lax.dynamic_index_in_dim(pattern, child_id, 0, keepdims=False)
    slot_ids = jnp.arange(SLOTS, dtype=jnp.int32)
    alive_slots = (slot_ids[None, :] < sizes_live[:, None]).astype(jnp.float32)
    within = jnp.arange(TILE, dtype=jnp.int32)
    row_offsets = lax.dynamic_slice_in_dim(offsets, row_start, row_groups, 0)
    col_offsets = lax.dynamic_slice_in_dim(offsets, block_start, block_groups, 0)
    row_tiles = (jnp.arange(row_groups, dtype=jnp.int32)[:, None] * GROUP + row_offsets).reshape(-1)
    col_tiles = (jnp.arange(block_groups, dtype=jnp.int32)[:, None] * GROUP + col_offsets).reshape(
        -1
    )
    row_indices = (row_tiles[:, None] * TILE + within[None, :]).reshape(-1)
    col_indices = (col_tiles[:, None] * TILE + within[None, :]).reshape(-1)
    picked = jnp.take(jnp.take(ancestor, row_indices, axis=0), col_indices, axis=1)
    row_alive = lax.dynamic_slice_in_dim(alive_slots, row_start, row_groups, 0).reshape(-1)
    col_alive = lax.dynamic_slice_in_dim(alive_slots, block_start, block_groups, 0).reshape(-1)
    row_slots = row_groups * SLOTS
    col_slots = block_groups * SLOTS
    pattern_block = lax.dynamic_slice(
        pattern_child, (row_start * SLOTS, block_start * SLOTS), (row_slots, col_slots)
    ).astype(jnp.float32)
    tile_mask = pattern_block * row_alive[:, None] * col_alive[None, :]
    shaped = picked.reshape(row_slots, TILE, col_slots, TILE) * tile_mask[:, None, :, None]
    return shaped.reshape(row_slots * TILE, col_slots * TILE)


def per_device(ancestor, panel, diag_inverse, frontier, counts, pattern):
    sec_index = lax.axis_index("sec")
    row_index = lax.axis_index("row")
    col_index = lax.axis_index("col")
    row_count = lax.axis_size("row")
    col_count = lax.axis_size("col")
    groups_all = frontier.shape[1]
    row_groups = groups_all // row_count
    block_groups = groups_all // (2 * col_count)
    own_block = sec_index * col_count + col_index
    row_start = row_index * row_groups
    block_start = own_block * block_groups
    mine = pick_tiles(
        ancestor,
        frontier,
        counts,
        pattern,
        sec_index,
        row_start,
        block_start,
        row_groups,
        block_groups,
    )
    theirs = pick_tiles(
        ancestor,
        frontier,
        counts,
        pattern,
        1 - sec_index,
        row_start,
        block_start,
        row_groups,
        block_groups,
    )
    partner = swapped(theirs, "sec", 0)
    leading = jnp.where(sec_index == 0, mine, partner)
    trailing = jnp.where(sec_index == 0, partner, mine)
    chosen = jnp.concatenate([leading, trailing], axis=1)
    rows_full = lax.all_gather(panel[0], "col", axis=1, tiled=True)
    take_groups = min(block_groups, row_groups)
    take_rows = take_groups * SLOTS * TILE
    starts = []
    for block_id in (col_index, col_count + col_index):
        starts.append(block_id * block_groups + 0)
    pieces = []
    for first_group in starts:
        received = from_root(rows_full, "row", first_group // row_groups)
        pieces.append(
            lax.dynamic_slice_in_dim(
                received, first_group % row_groups * SLOTS * TILE, take_rows, 0
            )
        )
    columns = jnp.concatenate(pieces, axis=0)
    cross_part = -lax.psum_scatter(
        lax.dot_general(
            columns,
            chosen,
            (((0,), (1,)), ((), ())),
            precision=lax.Precision.HIGHEST,
            preferred_element_type=jnp.float32,
        ),
        "col",
        scatter_dimension=0,
        tiled=True,
    )
    products = jnp.dot(
        cross_part, rows_full, precision=lax.Precision.HIGHEST, preferred_element_type=jnp.float32
    )
    summed = lax.psum_scatter(products, "row", scatter_dimension=1, tiled=True)
    inverse_part = diag_inverse[0] - summed
    return (cross_part[None], inverse_part[None])


def solution(mesh):
    return jax.shard_map(
        per_device,
        mesh=mesh,
        in_specs=(
            P("row", ("sec", "col")),
            P("sec", "row", "col"),
            P("sec", "col", "row"),
            P(),
            P(),
            P(),
        ),
        out_specs=(P("sec", "col", "row"), P("sec", "col", "row")),
        check_vma=False,
    )
```

profile of v0, /device:TPU:0, one launch (start us, length us, event | category | flops | bytes accessed | tf_op | source)
XLA Modules:
  0.0 1363.4 jit_solution(10710319041521073351)
XLA Ops:
  7.2 0.7 all-gather.3.cloned.1.call-update
  8.0 291.1 %all-gather.3.cloned.1.call-done = f32[1,2048,2048]{2,1,0:T(8,128)} async-done(((f32[1,2048,512]{2,1,0:T(8,128)}), f32[1,2048,2048]{2,1,0:T(8,128)}) %all-gather.3.cloned.1.call-update) | async-done | bytes 16777232 | tf_op jit(solution)/shard_map/all_gather | solution.py:90
  299.1 17.7 %bitcast_select_fusion.1 = (f32[2048,2048]{1,0:T(8,128)}, f32[2048,2048]{1,0:T(8,128)}) fusion(f32[1,2048,2048]{2,1,0:T(8,128)} %all-gather.3.cloned.1.call-done, pred[]{:T(512)S(6)} %eq.13, pred[]{:T(512)S(6)} %eq.14), kind=kLoop, calls=%fused_computation.14 | loop fusion | flops 8388608 | bytes 50331648 | tf_op jit(solution)/shard_map/jit(_where)/select_n | solution.py:18
  316.8 0.8 fusion.34
  317.8 0.1 mul.190
  317.9 0.1 mul.187
  318.1 0.1 add.227
  318.2 0.1 constant_dynamic-slice_fusion.9
  318.2 0.1 copy.9
  318.3 0.1 dynamic_slice.60
  318.4 0.1 copy.13
  318.5 0.1 dynamic_slice.68
  318.6 0.1 fusion.11
  318.7 28.5 %gather_fusion.2 = f32[2048,2048]{1,0:T(8,128)} fusion(f32[4096,2048]{1,0:T(8,128)} %param.10, s32[2048]{0:T(1024)S(1)} %get-tuple-element.26), kind=kCustom, calls=%fused_computation.2.clone | custom fusion | bytes 33562624 | tf_op jit(solution)/shard_map/jit(_take)/gather | solution.py:39
  347.2 0.1 fusion.17
  347.2 11.9 broadcast_select_fusion
  359.2 17.9 %copy.14 = f32[2048,2048]{0,1:T(8,128)} copy(f32[2048,2048]{1,0:T(8,128)} %broadcast_select_fusion) | data formatting | bytes 33554432 | tf_op jit(solution)/shard_map/jit(_take)/select_n | solution.py:39
  377.2 0.1 add.236
  377.3 0.1 copy.8
  377.4 0.1 dynamic_slice.62
  377.5 0.1 copy.12
  377.6 0.1 dynamic_slice.70
  377.7 0.1 fusion.23
  377.8 15.3 %gather_fusion.3 = f32[1024,2048]{1,0:T(8,128)} fusion(f32[2048,2048]{0,1:T(8,128)} %copy.14, s32[1024]{0:T(1024)S(1)} %fusion.23), kind=kCustom, calls=%fused_computation.3.clone | custom fusion | bytes 16781312 | tf_op jit(solution)/shard_map/jit(_take)/gather | solution.py:39
  393.1 0.1 fusion.30
  393.2 0.6 mul.193
  393.9 2.6 copy-done.1
  396.5 7.5 bitcast_multiply_fusion
  404.0 1.5 collective-permute-start
  405.5 0.1 mul.179
  405.6 0.1 mul.176
  405.7 27.4 %gather_fusion = f32[2048,2048]{1,0:T(8,128)} fusion(f32[4096,2048]{1,0:T(8,128)} %param.10, s32[2048]{0:T(1024)S(1)} %get-tuple-element.27), kind=kCustom, calls=%fused_computation.clone | custom fusion | bytes 33562624 | tf_op jit(solution)/shard_map/jit(_take)/gather | solution.py:39
  433.1 11.8 broadcast_select_fusion.1
  444.8 17.8 %copy.10 = f32[2048,2048]{0,1:T(8,128)} copy(f32[2048,2048]{1,0:T(8,128)} %broadcast_select_fusion.1) | data formatting | bytes 33554432 | tf_op jit(solution)/shard_map/jit(_take)/select_n | solution.py:39
  462.6 0.1 fusion.26
  462.6 14.9 %gather_fusion.1 = f32[1024,2048]{1,0:T(8,128)} fusion(f32[2048,2048]{0,1:T(8,128)} %copy.10, s32[1024]{0:T(1024)S(1)} %fusion.26), kind=kCustom, calls=%fused_computation.1.clone | custom fusion | bytes 16781312 | tf_op jit(solution)/shard_map/jit(_take)/gather | solution.py:39
  477.5 0.1 fusion.29
  477.7 108.7 %collective-permute-done = f32[2048,1024]{0,1:T(8,128)} collective-permute-done((f32[2048,1024]{0,1:T(8,128)}, f32[2048,1024]{0,1:T(8,128)}, u32[]{:S(2)}, u32[]{:S(2)}) %collective-permute-start) | collective-permute-done | bytes 8388640 | tf_op jit(solution)/shard_map/ppermute | solution.py:14
  586.4 3.9 mul.182
  590.3 13.7 %broadcast_select_fusion.3 = (f32[2048,1024]{0,1:T(8,128)}, f32[2048,1024]{0,1:T(8,128)}) fusion(f32[2048,1024]{0,1:T(8,128)} %collective-permute-done, pred[]{:T(512)S(6)} %eq.15, f32[128,8,16,128]{3,2,1,0:T(8,128)} %bitcast.97, f32[1024,2048]{1,0:T(8,128)S(1)} %copy-done, pred[1024]{0:T(1024)(128)(4,1)S(1)} %fusion.29), kind=kLoop, calls=%fused_computation.20 | loop fusion | flops 8388608 | bytes 41944064 | tf_op jit(solution)/shard_map/jit(_where)/select_n | solution.py:87
  604.0 270.1 %all-reduce.3.cloned.1.call-done = (f32[2048,2048]{1,0:T(8,128)}, f32[2048,2048]{1,0:T(8,128)}) async-done(((f32[2048,2048]{1,0:T(8,128)}, f32[2048,2048]{1,0:T(8,128)}), (f32[2048,2048]{1,0:T(8,128)}, f32[2048,2048]{1,0:T(8,128)})) %all-reduce.3.cloned.1.call-update) | async-done | bytes 33554448 | tf_op jit(solution)/shard_map/psum | solution.py:19
  874.1 10.8 constant_dynamic-slice_fusion.10
  885.0 111.7 %fusion = f32[2048,2048]{1,0:T(8,128)} fusion(f32[1024,2048]{1,0:T(8,128)} %get-tuple-element.22, f32[1024,2048]{1,0:T(8,128)} %get-tuple-element.23, f32[2048,1024]{0,1:T(8,128)} %get-tuple-element.7, f32[2048,1024]{0,1:T(8,128)} %get-tuple-element.6), kind=kOutput, calls=%fused_computation.4 | convolution fusion | flops 103087603712 | bytes 50331648 | tf_op jit(solution)/shard_map/dot_general | solution.py:106
  996.7 280.4 %reduce-scatter.3.cloned.1.call-done = f32[512,2048]{1,0:T(8,128)} async-done(((f32[2048,2048]{1,0:T(8,128)}), f32[512,2048]{1,0:T(8,128)}) %reduce-scatter.3.cloned.1.call-update) | async-done | bytes 4194320 | tf_op jit(solution)/shard_map/reduce_scatter | solution.py:105
  1277.1 32.0 %fusion.7 = f32[512,2048]{1,0:T(8,128)} fusion(f32[1,2048,2048]{2,1,0:T(8,128)} %all-gather.3.cloned.1.call-done, f32[512,2048]{1,0:T(8,128)} %reduce-scatter.3.cloned.1.call-done), kind=kOutput, calls=%fused_computation.11 | convolution fusion | flops 25770852352 | bytes 25165824 | tf_op jit(solution)/shard_map/dot_general | solution.py:117
  1309.1 4.9 negate_bitcast_fusion
  1314.0 40.5 %reduce-scatter.5.cloned.1.call-done = f32[512,512]{1,0:T(8,128)} async-done(((f32[512,2048]{1,0:T(8,128)}), f32[512,512]{1,0:T(8,128)}) %reduce-scatter.5.cloned.1.call-update) | async-done | bytes 1048592 | tf_op jit(solution)/shard_map/reduce_scatter | solution.py:120
  1354.5 2.4 fusion.10
  (33 shorter events, 0.8 us)
Async XLA Ops:
  7.2 291.9 %all-gather.3.cloned.1.call-start = ((), (), s32[]{:S(2)}) async-start(), calls=%async_computation.4 | async-start | bytes 20971520 | tf_op jit(solution)/shard_map/all_gather | solution.py:90
  7.9 866.2 %all-reduce.3.cloned.1.call-start = ((), (), s32[]{:S(2)}) async-start(), calls=%async_computation.5 | async-start | bytes 67108864 | tf_op jit(solution)/shard_map/psum | solution.py:19
  316.7 1.0 copy-start.4
  316.7 1.4 copy-start.3
  316.8 960.3 %reduce-scatter.3.cloned.1.call-start = ((), (), s32[]{:S(2)}) async-start(), calls=%async_computation.2 | async-start | bytes 20971520 | tf_op jit(solution)/shard_map/reduce_scatter | solution.py:105
  393.1 3.4 copy-start.1
  404.0 182.4 %collective-permute-start = (f32[2048,1024]{0,1:T(8,128)}, f32[2048,1024]{0,1:T(8,128)}, u32[]{:S(2)}, u32[]{:S(2)}) collective-permute-start(f32[2048,1024]{0,1:T(8,128)} %bitcast_multiply_fusion), channel_id=1, source_target_pairs={{0,16},{16,0},{1,17},{17,1},{2,18},{18,2},{3,19},{19,3},{4,20},{20... | collective-permute-start | bytes 25165832 | tf_op jit(solution)/shard_map/ppermute | solution.py:14
  477.5 112.8 %copy-start = (f32[1024,2048]{1,0:T(8,128)S(1)}, f32[1024,2048]{1,0:T(8,128)}, u32[]{:S(2)}) copy-start(f32[1024,2048]{1,0:T(8,128)} %gather_fusion.1) | copy-start | bytes 25165828
  996.6 357.9 %reduce-scatter.5.cloned.1.call-start = ((), (), s32[]{:S(2)}) async-start(), calls=%async_computation.3 | async-start | bytes 5242880 | tf_op jit(solution)/shard_map/reduce_scatter | solution.py:120
  1309.1 45.4 %copy-start.2 = (f32[1,512,512]{2,1,0:T(8,128)S(1)}, f32[1,512,512]{2,1,0:T(8,128)}, u32[]{:S(2)}) copy-start(f32[1,512,512]{2,1,0:T(8,128)} %param.12) | copy-start | bytes 3145732
Sparse Core Ops, SparseCore 0:
  9.6 289.4 all-gather.2
  316.9 557.2 all-reduce.2
  996.8 280.3 reduce-scatter.2
  1309.2 45.2 reduce-scatter.4
where the time goes:
time: 1360 us
  waiting for transfers between devices  992 us (73%)
  matrix products  144 us (11%)
  local copies, waits for them, and re-layouts  142 us (10%)
  other arithmetic  70.4 us (5%)
  between operations  13.9 us (1%)
    all_gather x1, waiting for transfers between devices, per_device(): rows_full = lax.all_gather(panel[0], 'col', axis=1, tiled=True)  291 us
    reduce_scatter x1, waiting for transfers between devices, per_device(): lax.psum_scatter(lax.dot_general(columns, chosen, (((0,), (1,)), ((), ())...  280 us
    psum x1, waiting for transfers between devices, from_root(): return lax.psum(kept, axis)  270 us
    dot_general x1, matrix products, per_device(): lax.dot_general(columns, chosen, (((0,), (1,)), ((), ())), precision=lax....  112 us
    ppermute x1, waiting for transfers between devices, swapped(): return lax.ppermute(value, axis, pairs)  109 us
    gather x2, local copies, waits for them, and re-layouts, pick_tiles(): jnp.take(ancestor, row_indices, axis=0)  55.8 us
    reduce_scatter x1, waiting for transfers between devices, per_device(): summed = lax.psum_scatter(products, 'row', scatter_dimension=1, tiled=True)  40.5 us
    select_n x2, local copies, waits for them, and re-layouts, pick_tiles(): jnp.take(ancestor, row_indices, axis=0)  35.7 us
  transfers between devices with their start and end apart: 5, of which 5 were waited for; matrix products, arithmetic and copies ran while one was open for 13% of the time, Pallas kernels for 0%

commit v1 on v0

v1 whole, which is shorter than its diff:
```python
import functools

import jax
import jax.numpy as jnp
from jax import lax
from jax.experimental import pallas as pl
from jax.experimental.pallas import tpu as pltpu
from jax.sharding import PartitionSpec as P

TILE = 128
GROUP = 8
SLOTS = 4


def pick_kernel(col_slots, row_tiles, col_tiles, mask, strip, out):
    i = pl.program_id(0)
    for j in range(col_slots):
        start = pl.multiple_of(col_tiles[j] * TILE, TILE)
        tile = strip[:, pl.ds(start, TILE)]
        out[:, j * TILE : (j + 1) * TILE] = jnp.where(mask[i * col_slots + j] != 0, -tile, 0.0)


def pick_tiles(
    ancestor, frontier, counts, pattern, child_id, row_start, block_start, row_groups, block_groups
):
    offsets = lax.dynamic_index_in_dim(frontier, child_id, 0, keepdims=False)
    sizes_live = lax.dynamic_index_in_dim(counts, child_id, 0, keepdims=False)
    pattern_child = lax.dynamic_index_in_dim(pattern, child_id, 0, keepdims=False)
    alive = (jnp.arange(SLOTS, dtype=jnp.int32)[None, :] < sizes_live[:, None]).astype(jnp.int32)
    row_offsets = lax.dynamic_slice_in_dim(offsets, row_start, row_groups, 0)
    col_offsets = lax.dynamic_slice_in_dim(offsets, block_start, block_groups, 0)
    row_tiles = (jnp.arange(row_groups, dtype=jnp.int32)[:, None] * GROUP + row_offsets).reshape(-1)
    col_tiles = (jnp.arange(block_groups, dtype=jnp.int32)[:, None] * GROUP + col_offsets).reshape(
        -1
    )
    row_alive = lax.dynamic_slice_in_dim(alive, row_start, row_groups, 0).reshape(-1)
    col_alive = lax.dynamic_slice_in_dim(alive, block_start, block_groups, 0).reshape(-1)
    row_slots = row_groups * SLOTS
    col_slots = block_groups * SLOTS
    pattern_block = lax.dynamic_slice(
        pattern_child, (row_start * SLOTS, block_start * SLOTS), (row_slots, col_slots)
    )
    mask = (pattern_block * row_alive[:, None] * col_alive[None, :]).reshape(-1)
    width = ancestor.shape[1]
    return pl.pallas_call(
        functools.partial(pick_kernel, col_slots),
        out_shape=jax.ShapeDtypeStruct((row_slots * TILE, col_slots * TILE), jnp.float32),
        grid_spec=pltpu.PrefetchScalarGridSpec(
            num_scalar_prefetch=3,
            grid=(row_slots,),
            in_specs=[pl.BlockSpec((TILE, width), lambda i, rows, cols, kept: (rows[i], 0))],
            out_specs=pl.BlockSpec((TILE, col_slots * TILE), lambda i, rows, cols, kept: (i, 0)),
        ),
        cost_estimate=pl.CostEstimate(
            flops=0,
            bytes_accessed=row_slots * TILE * (width + col_slots * TILE) * 4,
            transcendentals=0,
        ),
    )(row_tiles, col_tiles, mask, ancestor)


def dot_high(left, right, dims):
    return lax.dot_general(
        left,
        right,
        (dims, ((), ())),
        precision=lax.Precision.HIGH,
        preferred_element_type=jnp.float32,
    )


def per_device(ancestor, panel, diag_inverse, frontier, counts, pattern):
    sec_index = lax.axis_index("sec")
    row_index = lax.axis_index("row")
    col_index = lax.axis_index("col")
    row_count = lax.axis_size("row")
    col_count = lax.axis_size("col")
    groups_all = frontier.shape[1]
    row_groups = groups_all // row_count
    block_groups = groups_all // (2 * col_count)
    row_start = row_index * row_groups
    block_start = (sec_index * col_count + col_index) * block_groups
    pick = functools.partial(
        pick_tiles,
        ancestor,
        frontier,
        counts,
        pattern,
        row_start=row_start,
        block_start=block_start,
        row_groups=row_groups,
        block_groups=block_groups,
    )
    theirs = pick(child_id=1 - sec_index)
    partner = lax.ppermute(theirs, "sec", [(0, 1), (1, 0)])
    mine = pick(child_id=sec_index)

    ring = [(c, (c + 1) % col_count) for c in range(col_count)]
    take_rows = block_groups * SLOTS * TILE
    width = panel.shape[2]
    top = row_count // 2
    slot_start = col_index * block_groups % row_groups * SLOTS * TILE
    holders = [c * block_groups // row_groups for c in range(col_count)]
    holder = col_index * block_groups // row_groups
    lead_is_own = ((row_index & top) == 0) == (sec_index == 0)

    def share_in_plane(block):
        part = lax.dynamic_slice_in_dim(block, slot_start, take_rows, 0)
        known = {(c, holders[c] ^ flip) for c in range(col_count) for flip in (0, top)}

        def pairs(bit):
            return sorted((c * row_count + r, c * row_count + (r ^ bit)) for c, r in known)

        other = lax.ppermute(part, ("col", "row"), pairs(top))
        lead = jnp.where(lead_is_own, part, other)
        trail = jnp.where(lead_is_own, other, part)
        bit = top // 2
        while bit:
            got_lead = lax.ppermute(lead, ("col", "row"), pairs(bit))
            got_trail = lax.ppermute(trail, ("col", "row"), pairs(bit))
            fresh = ((row_index ^ holder) & (2 * bit - 1)) == bit
            lead = jnp.where(fresh, got_lead, lead)
            trail = jnp.where(fresh, got_trail, trail)
            known |= {(c, r ^ bit) for c, r in known}
            bit //= 2
        return lead, trail

    blocks = [panel[0]]
    for _ in range(col_count - 1):
        blocks.append(lax.ppermute(blocks[-1], "col", ring))

    def term(block):
        lead, trail = share_in_plane(block)
        return dot_high(lead, mine, ((0,), (1,))) + dot_high(trail, partner, ((0,), (1,)))

    total = term(blocks[1])
    for step in range(2, col_count):
        total = lax.ppermute(total, "col", ring) + term(blocks[step])
    cross_part = lax.ppermute(total, "col", ring) + term(blocks[0])

    rows_full = jnp.zeros((panel.shape[1], width * col_count), jnp.float32)
    for step in range(col_count):
        owner = (col_index - step) % col_count
        rows_full = lax.dynamic_update_slice_in_dim(rows_full, blocks[step], owner * width, 1)
    summed = dot_high(cross_part, rows_full, ((1,), (0,)))
    out_width = diag_inverse.shape[2]
    summed = summed.reshape(width, row_count, out_width)
    bit = 1
    while bit < row_count:
        halves = summed.reshape(width, -1, 2, out_width)
        side = row_index // bit % 2
        kept = lax.dynamic_index_in_dim(halves, side, 2, keepdims=False)
        sent = lax.dynamic_index_in_dim(halves, 1 - side, 2, keepdims=False)
        summed = kept + lax.ppermute(sent, "row", [(r, r ^ bit) for r in range(row_count)])
        bit *= 2
    inverse_part = diag_inverse[0] - summed.reshape(width, out_width)
    return (cross_part[None], inverse_part[None])


def solution(mesh):
    return jax.shard_map(
        per_device,
        mesh=mesh,
        in_specs=(
            P("row", ("sec", "col")),
            P("sec", "row", "col"),
            P("sec", "col", "row"),
            P(),
            P(),
            P(),
        ),
        out_specs=(P("sec", "col", "row"), P("sec", "col", "row")),
        check_vma=False,
    )
```

time: 1360 us -> 650 us (0.48)
  waiting for transfers between devices: 992 us -> 337 us
  local copies, waits for them, and re-layouts: 142 us -> 58.9 us
  other arithmetic: 70.4 us -> 36.8 us
  starting transfers between devices: 1.64 us -> 34.3 us
  Pallas kernels: 0 us -> 30.4 us
    reduce_scatter x2 -> x0, waiting for transfers between devices: 321 us -> none  [the longest x1 280 us: per_device(): lax.psum_scatter(lax.dot_general(columns, chosen, (((0,), (1,)), ((), ())...]
    all_gather x1 -> x0, waiting for transfers between devices: 291 us -> none  [per_device(): rows_full = lax.all_gather(panel[0], 'col', axis=1, tiled=True)]
    psum x1 -> x0, waiting for transfers between devices: 270 us -> none  [from_root(): return lax.psum(kept, axis)]
    ppermute x1 -> x21, waiting for transfers between devices: 109 us -> 337 us  [the longest x3 166 us: per_device(): blocks.append(lax.ppermute(blocks[-1], 'col', ring))]
    gather x4 -> x0, local copies, waits for them, and re-layouts: 86 us -> none  [the longest x2 55.8 us: pick_tiles(): jnp.take(ancestor, row_indices, axis=0)]
    select_n x4, other arithmetic: 55 us -> 11.3 us  [the longest x3 7.3 us: share_in_plane(): trail = jnp.where(lead_is_own, other, part)]
    select_n x2 -> x0, local copies, waits for them, and re-layouts: 35.7 us -> none  [pick_tiles(): jnp.take(ancestor, row_indices, axis=0)]
    ppermute x1 -> x21, starting transfers between devices: 1.48 us -> 34.3 us  [the longest x4 12.5 us: share_in_plane(): other = lax.ppermute(part, ('col', 'row'), pairs(top))]
  transfers between devices with their start and end apart: 5 -> 21, of which waited for: 5 -> 10; matrix products, arithmetic and copies ran while one was open for 13% -> 31% of each run, Pallas kernels for 0% -> 5%
where the time goes in v1:
time: 650 us; the launch traced here: 641 us
  waiting for transfers between devices  337 us (52%)
  matrix products  143 us (22%)
  local copies, waits for them, and re-layouts  58.9 us (9%)
  other arithmetic  36.8 us (6%)
  starting transfers between devices  34.3 us (5%)
  Pallas kernels  30.4 us (5%)
    ppermute x3, waiting for transfers between devices, per_device(): blocks.append(lax.ppermute(blocks[-1], 'col', ring))  166 us
    dot_general x9, matrix products, dot_high(): lax.dot_general(left, right, (dims, ((), ())), precision=lax.Precision.HI...  143 us
    ppermute x2, waiting for transfers between devices, per_device(): total = lax.ppermute(total, 'col', ring) + term(blocks[step])  78.2 us
    ppermute x4, waiting for transfers between devices, share_in_plane(): other = lax.ppermute(part, ('col', 'row'), pairs(top))  44 us
    pallas_call x2, Pallas kernels, pick_tiles(): pl.pallas_call(functools.partial(pick_kernel, col_slots), out_shape=jax.S...  30.4 us
    ppermute x1, waiting for transfers between devices, per_device(): cross_part = lax.ppermute(total, 'col', ring) + term(blocks[0])  29 us
    dynamic_update_slice x4, local copies, waits for them, and re-layouts, per_device(): lax.dynamic_update_slice_in_dim(rows_full, blocks[step], owner * width, 1)  19.8 us
    ppermute x2, waiting for transfers between devices, per_device(): lax.ppermute(sent, 'row', [(r, r ^ bit) for r in range(row_count)])  19.7 us
  transfers between devices with their start and end apart: 21, of which 10 were waited for; matrix products, arithmetic and copies ran while one was open for 31% of the time, Pallas kernels for 5%

profile of v1, /device:TPU:0, one launch (start us, length us, event | category | flops | bytes accessed | tf_op | source)
XLA Modules:
  0.0 641.4 jit_solution(5195893991673203668)
XLA Ops:
  0.6 3.1 collective-permute-start
  10.1 15.6 %shard_map.78 = f32[2048,1024]{1,0:T(8,128)} custom-call(s32[16]{0:T(128)} %get-tuple-element.23.row_tiles, s32[8]{0:T(128)} %get-tuple-element.21.col_tiles, s32[128]{0:T(128)} %multiply_multiply_fusion.mask, f32[4096,2048]{1,0:T(8,128)} %strip.3), custom_call_target="tpu_custom_call" | custom-call | bytes 25165824 | tf_op jit(solution)/shard_map/pallas_call | solution.py:45
  27.2 69.4 %collective-permute-done = f32[2048,512]{1,0:T(8,128)} collective-permute-done((f32[2048,512]{1,0:T(8,128)}, f32[2048,512]{1,0:T(8,128)}, u32[]{:S(2)}, u32[]{:S(2)}) %collective-permute-start) | collective-permute-done | bytes 4194336 | tf_op jit(solution)/shard_map/ppermute | solution.py:130
  96.6 1.8 constant_dynamic-slice_fusion.15
  98.4 3.4 collective-permute-start.1
  101.8 24.6 %collective-permute-done.1 = f32[1024,512]{1,0:T(8,128)} collective-permute-done((f32[1024,512]{1,0:T(8,128)S(1)}, f32[1024,512]{1,0:T(8,128)}, u32[]{:S(2)}, u32[]{:S(2)}) %collective-permute-start.1) | collective-permute-done | bytes 2097184 | tf_op jit(solution)/shard_map/ppermute | solution.py:114
  126.5 4.0 broadcast_select_fusion.7
  130.5 2.6 collective-permute-start.3
  133.1 2.6 collective-permute-start.2
  135.7 54.8 %collective-permute-done.6 = f32[2048,512]{1,0:T(8,128)} collective-permute-done((f32[2048,512]{1,0:T(8,128)}, f32[2048,512]{1,0:T(8,128)}, u32[]{:S(2)}, u32[]{:S(2)}) %collective-permute-start.6) | collective-permute-done | bytes 4194336 | tf_op jit(solution)/shard_map/ppermute | solution.py:130
  190.5 3.1 constant_dynamic-slice_fusion.4
  193.6 3.1 collective-permute-start.7
  197.9 14.8 %shard_map.77 = f32[2048,1024]{1,0:T(8,128)} custom-call(s32[16]{0:T(128)} %get-tuple-element.22.row_tiles, s32[8]{0:T(128)} %get-tuple-element.20.col_tiles, s32[128]{0:T(128)} %multiply_multiply_fusion.1.mask, f32[4096,2048]{1,0:T(8,128)} %strip.3), custom_call_target="tpu_custom_call" | custom-call | bytes 25165824 | tf_op jit(solution)/shard_map/pallas_call | solution.py:45
  212.7 16.6 %fusion.12 = f32[512,2048]{1,0:T(8,128)S(1)} fusion(f32[2048,1024]{1,0:T(8,128)} %collective-permute-done.4, f32[1024,512]{1,0:T(8,128)} %collective-permute-done.3, f32[1024,512]{1,0:T(8,128)} %get-tuple-element.11, pred[]{:T(512)S(6)} %eq.23), kind=kOutput, calls=%fused_computation.19 | convolution fusion | flops 6442975232 | bytes 16777216 | tf_op jit(solution)/shard_map/dot_general | solution.py:63
  229.3 16.2 %convolution_add_fusion = f32[512,2048]{1,0:T(8,128)} fusion(f32[512,2048]{1,0:T(8,128)S(1)} %fusion.12, f32[2048,1024]{1,0:T(8,128)S(1)} %copy-done, f32[1024,512]{1,0:T(8,128)} %collective-permute-done.2, f32[1024,512]{1,0:T(8,128)S(1)} %get-tuple-element.10, pred[]{:T(512)S(6)} %eq.23), kind=kOutput, calls=%fused_computation.3 | convolution fusion | flops 6444023808 | bytes 20971520 | tf_op jit(solution)/shard_map/dot_general | solution.py:63
  245.4 2.7 broadcast_select_fusion.4
  251.0 41.9 %collective-permute-done.11 = f32[2048,512]{1,0:T(8,128)} collective-permute-done((f32[2048,512]{1,0:T(8,128)}, f32[2048,512]{1,0:T(8,128)}, u32[]{:S(2)}, u32[]{:S(2)}) %collective-permute-start.11) | collective-permute-done | bytes 4194336 | tf_op jit(solution)/shard_map/ppermute | solution.py:130
  292.9 3.1 constant_dynamic-slice_fusion.3
  296.1 3.1 collective-permute-start.12
  299.2 13.9 %fusion.10 = f32[512,2048]{1,0:T(8,128)S(1)} fusion(f32[2048,1024]{1,0:T(8,128)S(1)} %copy-done, f32[1024,512]{1,0:T(8,128)S(1)} %collective-permute-done.8, f32[1024,512]{1,0:T(8,128)S(1)} %get-tuple-element.9, pred[]{:T(512)S(6)} %eq.23), kind=kOutput, calls=%fused_computation.17 | convolution fusion | flops 6442975232 | bytes 16777216 | tf_op jit(solution)/shard_map/dot_general | solution.py:63
  313.1 15.8 %fusion.8 = f32[512,2048]{1,0:T(8,128)S(1)} fusion(f32[2048,1024]{1,0:T(8,128)} %collective-permute-done.4, f32[1024,512]{1,0:T(8,128)S(1)} %collective-permute-done.9, f32[1024,512]{1,0:T(8,128)S(1)} %get-tuple-element.8, pred[]{:T(512)S(6)} %eq.23), kind=kOutput, calls=%fused_computation.15 | convolution fusion | flops 6442975232 | bytes 16777216 | tf_op jit(solution)/shard_map/dot_general | solution.py:63
  329.0 50.1 %collective-permute-done.5 = f32[512,2048]{1,0:T(8,128)} collective-permute-done((f32[512,2048]{1,0:T(8,128)}, f32[512,2048]{1,0:T(8,128)}, u32[]{:S(2)}, u32[]{:S(2)}) %collective-permute-start.5) | collective-permute-done | bytes 4194336 | tf_op jit(solution)/shard_map/ppermute | solution.py:138
  379.0 5.6 add_add_fusion.2
  384.8 2.9 collective-permute-start.16
  387.8 2.7 broadcast_select_fusion.2
  393.4 19.4 %collective-permute-done.16 = f32[1024,512]{1,0:T(8,128)S(1)} collective-permute-done((f32[1024,512]{1,0:T(8,128)S(1)}, f32[1024,512]{1,0:T(8,128)S(1)}, u32[]{:S(2)}, u32[]{:S(2)}) %collective-permute-start.16) | collective-permute-done | bytes 2097184 | tf_op jit(solution)/shard_map/ppermute | solution.py:114
  412.8 1.8 broadcast_select_fusion
  414.6 2.8 collective-permute-start.17
  417.5 14.2 %fusion.6 = f32[512,2048]{1,0:T(8,128)S(1)} fusion(f32[2048,1024]{1,0:T(8,128)S(1)} %copy-done, f32[1024,512]{1,0:T(8,128)S(1)} %collective-permute-done.13, f32[1024,512]{1,0:T(8,128)S(1)} %get-tuple-element.7, pred[]{:T(512)S(6)} %eq.23), kind=kOutput, calls=%fused_computation.13 | convolution fusion | flops 6442975232 | bytes 16777216 | tf_op jit(solution)/shard_map/dot_general | solution.py:63
  431.6 15.8 %fusion.4 = f32[512,2048]{1,0:T(8,128)S(1)} fusion(f32[2048,1024]{1,0:T(8,128)} %collective-permute-done.4, f32[1024,512]{1,0:T(8,128)S(1)} %collective-permute-done.14, f32[1024,512]{1,0:T(8,128)S(1)} %get-tuple-element.6, pred[]{:T(512)S(6)} %eq.23), kind=kOutput, calls=%fused_computation.11 | convolution fusion | flops 6442975232 | bytes 16777216 | tf_op jit(solution)/shard_map/dot_general | solution.py:63
  447.5 28.1 %collective-permute-done.10 = f32[512,2048]{1,0:T(8,128)} collective-permute-done((f32[512,2048]{1,0:T(8,128)}, f32[512,2048]{1,0:T(8,128)}, u32[]{:S(2)}, u32[]{:S(2)}) %collective-permute-start.10) | collective-permute-done | bytes 4194336 | tf_op jit(solution)/shard_map/ppermute | solution.py:138
  475.6 5.6 add_add_fusion.1
  481.2 1.8 collective-permute-start.18
  483.1 7.9 %broadcast_in_dim.5 = f32[2048,2048]{1,0:T(8,128)} broadcast(f32[]{:T(128)} %constant.239.clone.1), dimensions={} | broadcast | bytes 16777220 | tf_op jit(solution)/shard_map/broadcast_in_dim | solution.py:141
  491.0 2.6 constant_dynamic-update-slice_fusion.3
  493.5 4.9 constant_dynamic-update-slice_fusion.2
  498.4 15.4 %fusion.2 = f32[512,2048]{1,0:T(8,128)S(1)} fusion(f32[2048,1024]{1,0:T(8,128)S(1)} %bitcast.29, f32[1024,512]{1,0:T(8,128)} %collective-permute-done.17, f32[1024,512]{1,0:T(8,128)} %get-tuple-element.5, pred[]{:T(512)S(6)} %eq.23), kind=kOutput, calls=%fused_computation.8 | convolution fusion | flops 6442975232 | bytes 16777216 | tf_op jit(solution)/shard_map/dot_general | solution.py:63
  513.9 6.2 constant_dynamic-update-slice_fusion.1
  520.1 15.9 %fusion = f32[512,2048]{1,0:T(8,128)S(1)} fusion(f32[2048,1024]{1,0:T(8,128)} %collective-permute-done.4, f32[1024,512]{1,0:T(8,128)S(1)} %collective-permute-done.18, f32[1024,512]{1,0:T(8,128)S(1)} %get-tuple-element.4, pred[]{:T(512)S(6)} %eq.23), kind=kOutput, calls=%fused_computation.6 | convolution fusion | flops 6442975232 | bytes 16777216 | tf_op jit(solution)/shard_map/dot_general | solution.py:63
  536.1 6.1 constant_dynamic-update-slice_fusion
  542.2 29.0 %collective-permute-done.15 = f32[512,2048]{1,0:T(8,128)} collective-permute-done((f32[512,2048]{1,0:T(8,128)}, f32[512,2048]{1,0:T(8,128)}, u32[]{:S(2)}, u32[]{:S(2)}) %collective-permute-start.15) | collective-permute-done | bytes 4194336 | tf_op jit(solution)/shard_map/ppermute | solution.py:139
  571.2 18.7 %fusion.27 = f32[512,2048]{1,0:T(8,128)} fusion(f32[2048,2048]{1,0:T(8,128)} %constant_dynamic-update-slice_fusion, f32[512,2048]{1,0:T(8,128)} %collective-permute-done.15, f32[512,2048]{1,0:T(8,128)S(1)} %fusion.2, f32[512,2048]{1,0:T(8,128)S(1)} %fusion), kind=kOutput, calls=%fused_computation.69 | convolution fusion | flops 12886999040 | bytes 33554432 | tf_op jit(solution)/shard_map/dot_general | solution.py:63
  589.9 6.9 %reshape_reshape.3 = f32[512,2,2,512]{3,2,1,0:T(2,128)} reshape(f32[512,2048]{1,0:T(8,128)} %fusion.27) | data formatting | bytes 8388608 | tf_op jit(solution)/shard_map/reshape;reshape | solution.py:150
  596.8 7.8 %constant_dynamic-slice_fusion.2 = (f32[512,2,1,512]{3,2,1,0:T(1,128)S(1)}, f32[512,2,1,512]{3,2,1,0:T(1,128)S(1)}) fusion(f32[512,2,2,512]{3,2,1,0:T(2,128)} %reshape_reshape.3, s32[]{:T(128)S(6)} %select_n.228, s32[]{:T(128)S(6)} %select_n.229), kind=kLoop, calls=%fused_computation.45 | loop fusion | bytes 8388616 | tf_op jit(solution)/shard_map/jit(dynamic_index_in_dim)/dynamic_slice | solution.py:152
  606.3 4.5 collective-permute-done.19
  610.8 2.1 bitcast_add_fusion
  615.9 8.5 %fusion.28 = f32[1,512,2048]{2,1,0:T(8,128)} fusion(f32[512,2048]{1,0:T(8,128)} %collective-permute-done.15, f32[512,2048]{1,0:T(8,128)} %copy-done.3, f32[512,2048]{1,0:T(8,128)} %copy-done.4), kind=kLoop, calls=%fused_computation.70 | loop fusion | flops 2097152 | bytes 16777216 | tf_op jit(solution)/shard_map/broadcast_in_dim | solution.py:157
  624.4 15.2 %collective-permute-done.20 = f32[512,1,512]{2,0,1:T(8,128)S(1)} collective-permute-done((f32[512,1,512]{2,0,1:T(8,128)S(1)}, f32[512,1,512]{2,0,1:T(8,128)S(1)}, u32[]{:S(2)}, u32[]{:S(2)}) %collective-permute-start.20) | collective-permute-done | bytes 1048608 | tf_op jit(solution)/shard_map/ppermute | solution.py:154
  (88 shorter events, 20.9 us)
Async XLA Ops:
  0.6 96.0 %collective-permute-start = (f32[2048,512]{1,0:T(8,128)}, f32[2048,512]{1,0:T(8,128)}, u32[]{:S(2)}, u32[]{:S(2)}) collective-permute-start(f32[2048,512]{1,0:T(8,128)} %bitcast.30), channel_id=1, source_target_pairs={{0,4},{4,8},{8,12},{12,0},{1,5},{5,9},{9,13},{13,1},{2,6},{6,10},{... | collective-permute-start | bytes 12582920 | tf_op jit(solution)/shard_map/ppermute | solution.py:130
  25.7 187.0 %collective-permute-start.4 = (f32[2048,1024]{1,0:T(8,128)}, f32[2048,1024]{1,0:T(8,128)}, u32[]{:S(2)}, u32[]{:S(2)}) collective-permute-start(f32[2048,1024]{1,0:T(8,128)} %shard_map.78), channel_id=1, source_target_pairs={{0,16},{16,0},{1,17},{17,1},{2,18},{18,2},{3,19},{19,3},{4,20},{20... | collective-permute-start | bytes 25165832 | tf_op jit(solution)/shard_map/ppermute | solution.py:95
  96.6 93.9 %collective-permute-start.6 = (f32[2048,512]{1,0:T(8,128)}, f32[2048,512]{1,0:T(8,128)}, u32[]{:S(2)}, u32[]{:S(2)}) collective-permute-start(f32[2048,512]{1,0:T(8,128)} %collective-permute-done), channel_id=1, source_target_pairs={{0,4},{4,8},{8,12},{12,0},{1,5},{5,9},{9,13},{13,1},{2,6},{6,10},{... | collective-permute-start | bytes 12582920 | tf_op jit(solution)/shard_map/ppermute | solution.py:130
  98.4 28.0 %collective-permute-start.1 = (f32[1024,512]{1,0:T(8,128)S(1)}, f32[1024,512]{1,0:T(8,128)}, u32[]{:S(2)}, u32[]{:S(2)}) collective-permute-start(f32[1024,512]{1,0:T(8,128)S(1)} %constant_dynamic-slice_fusion.15), channel_id=1, source_target_pairs={{0,2},{2,0},{4,6},{6,4},{9,11},{11,9},{13,15},{15,13},{16,18},{18,... | collective-permute-start | bytes 6291464 | tf_op jit(solution)/shard_map/ppermute | solution.py:114
  130.5 82.2 %collective-permute-start.3 = (f32[1024,512]{1,0:T(8,128)}, f32[1024,512]{1,0:T(8,128)}, u32[]{:S(2)}, u32[]{:S(2)}) collective-permute-start(f32[1024,512]{1,0:T(8,128)} %get-tuple-element.11), channel_id=1, source_target_pairs={{0,1},{2,3},{4,5},{6,7},{9,8},{11,10},{13,12},{15,14},{16,17},{18,... | collective-permute-start | bytes 6291464 | tf_op jit(solution)/shard_map/ppermute | solution.py:120
  133.1 96.2 %collective-permute-start.2 = (f32[1024,512]{1,0:T(8,128)S(1)}, f32[1024,512]{1,0:T(8,128)}, u32[]{:S(2)}, u32[]{:S(2)}) collective-permute-start(f32[1024,512]{1,0:T(8,128)S(1)} %get-tuple-element.10), channel_id=1, source_target_pairs={{0,1},{2,3},{4,5},{6,7},{9,8},{11,10},{13,12},{15,14},{16,17},{18,... | collective-permute-start | bytes 6291464 | tf_op jit(solution)/shard_map/ppermute | solution.py:119
  193.6 51.8 %collective-permute-start.7 = (f32[1024,512]{1,0:T(8,128)}, f32[1024,512]{1,0:T(8,128)}, u32[]{:S(2)}, u32[]{:S(2)}) collective-permute-start(f32[1024,512]{1,0:T(8,128)} %constant_dynamic-slice_fusion.4), channel_id=1, source_target_pairs={{0,2},{2,0},{4,6},{6,4},{9,11},{11,9},{13,15},{15,13},{16,18},{18,... | collective-permute-start | bytes 6291464 | tf_op jit(solution)/shard_map/ppermute | solution.py:114
  197.3 95.7 %collective-permute-start.11 = (f32[2048,512]{1,0:T(8,128)}, f32[2048,512]{1,0:T(8,128)}, u32[]{:S(2)}, u32[]{:S(2)}) collective-permute-start(f32[2048,512]{1,0:T(8,128)} %collective-permute-done.6), channel_id=1, source_target_pairs={{0,4},{4,8},{8,12},{12,0},{1,5},{5,9},{9,13},{13,1},{2,6},{6,10},{... | collective-permute-start | bytes 12582920 | tf_op jit(solution)/shard_map/ppermute | solution.py:130
  212.7 16.6 %copy-start = (f32[2048,1024]{1,0:T(8,128)S(1)}, f32[2048,1024]{1,0:T(8,128)}, u32[]{:S(2)}) copy-start(f32[2048,1024]{1,0:T(8,128)} %shard_map.77) | copy-start | bytes 25165828
  245.4 133.6 %collective-permute-start.5 = (f32[512,2048]{1,0:T(8,128)}, f32[512,2048]{1,0:T(8,128)}, u32[]{:S(2)}, u32[]{:S(2)}) collective-permute-start(f32[512,2048]{1,0:T(8,128)} %convolution_add_fusion), channel_id=1, source_target_pairs={{0,4},{4,8},{8,12},{12,0},{1,5},{5,9},{9,13},{13,1},{2,6},{6,10},{... | collective-permute-start | bytes 12582920 | tf_op jit(solution)/shard_map/ppermute | solution.py:138
  248.2 51.0 %collective-permute-start.8 = (f32[1024,512]{1,0:T(8,128)S(1)}, f32[1024,512]{1,0:T(8,128)S(1)}, u32[]{:S(2)}, u32[]{:S(2)}) collective-permute-start(f32[1024,512]{1,0:T(8,128)S(1)} %get-tuple-element.9), channel_id=1, source_target_pairs={{0,1},{2,3},{4,5},{6,7},{9,8},{11,10},{13,12},{15,14},{16,17},{18,... | collective-permute-start | bytes 6291464 | tf_op jit(solution)/shard_map/ppermute | solution.py:119
  249.6 63.5 %collective-permute-start.9 = (f32[1024,512]{1,0:T(8,128)S(1)}, f32[1024,512]{1,0:T(8,128)S(1)}, u32[]{:S(2)}, u32[]{:S(2)}) collective-permute-start(f32[1024,512]{1,0:T(8,128)S(1)} %get-tuple-element.8), channel_id=1, source_target_pairs={{0,1},{2,3},{4,5},{6,7},{9,8},{11,10},{13,12},{15,14},{16,17},{18,... | collective-permute-start | bytes 6291464 | tf_op jit(solution)/shard_map/ppermute | solution.py:120
  296.1 91.7 %collective-permute-start.12 = (f32[1024,512]{1,0:T(8,128)}, f32[1024,512]{1,0:T(8,128)}, u32[]{:S(2)}, u32[]{:S(2)}) collective-permute-start(f32[1024,512]{1,0:T(8,128)} %constant_dynamic-slice_fusion.3), channel_id=1, source_target_pairs={{0,2},{2,0},{4,6},{6,4},{9,11},{11,9},{13,15},{15,13},{16,18},{18,... | collective-permute-start | bytes 6291464 | tf_op jit(solution)/shard_map/ppermute | solution.py:114
  329.0 55.7 %copy-start.1 = (f32[1,2048,512]{2,1,0:T(8,128)S(1)}, f32[1,2048,512]{2,1,0:T(8,128)}, u32[]{:S(2)}) copy-start(f32[1,2048,512]{2,1,0:T(8,128)} %param.7) | copy-start | bytes 12582916
  384.7 90.9 %collective-permute-start.10 = (f32[512,2048]{1,0:T(8,128)}, f32[512,2048]{1,0:T(8,128)}, u32[]{:S(2)}, u32[]{:S(2)}) collective-permute-start(f32[512,2048]{1,0:T(8,128)} %add_add_fusion.2), channel_id=1, source_target_pairs={{0,4},{4,8},{8,12},{12,0},{1,5},{5,9},{9,13},{13,1},{2,6},{6,10},{... | collective-permute-start | bytes 12582920 | tf_op jit(solution)/shard_map/ppermute | solution.py:138
  384.8 27.9 %collective-permute-start.16 = (f32[1024,512]{1,0:T(8,128)S(1)}, f32[1024,512]{1,0:T(8,128)S(1)}, u32[]{:S(2)}, u32[]{:S(2)}) collective-permute-start(f32[1024,512]{1,0:T(8,128)S(1)} %dynamic-slice_bitcast_fusion), channel_id=1, source_target_pairs={{0,2},{2,0},{4,6},{6,4},{9,11},{11,9},{13,15},{15,13},{16,18},{18,... | collective-permute-start | bytes 6291464 | tf_op jit(solution)/shard_map/ppermute | solution.py:114
  390.5 26.9 %collective-permute-start.13 = (f32[1024,512]{1,0:T(8,128)S(1)}, f32[1024,512]{1,0:T(8,128)S(1)}, u32[]{:S(2)}, u32[]{:S(2)}) collective-permute-start(f32[1024,512]{1,0:T(8,128)S(1)} %get-tuple-element.7), channel_id=1, source_target_pairs={{0,1},{2,3},{4,5},{6,7},{9,8},{11,10},{13,12},{15,14},{16,17},{18,... | collective-permute-start | bytes 6291464 | tf_op jit(solution)/shard_map/ppermute | solution.py:119
  392.0 39.7 %collective-permute-start.14 = (f32[1024,512]{1,0:T(8,128)S(1)}, f32[1024,512]{1,0:T(8,128)S(1)}, u32[]{:S(2)}, u32[]{:S(2)}) collective-permute-start(f32[1024,512]{1,0:T(8,128)S(1)} %get-tuple-element.6), channel_id=1, source_target_pairs={{0,1},{2,3},{4,5},{6,7},{9,8},{11,10},{13,12},{15,14},{16,17},{18,... | collective-permute-start | bytes 6291464 | tf_op jit(solution)/shard_map/ppermute | solution.py:120
  414.6 83.8 %collective-permute-start.17 = (f32[1024,512]{1,0:T(8,128)}, f32[1024,512]{1,0:T(8,128)}, u32[]{:S(2)}, u32[]{:S(2)}) collective-permute-start(f32[1024,512]{1,0:T(8,128)} %get-tuple-element.5), channel_id=1, source_target_pairs={{0,1},{2,3},{4,5},{6,7},{9,8},{11,10},{13,12},{15,14},{16,17},{18,... | collective-permute-start | bytes 6291464 | tf_op jit(solution)/shard_map/ppermute | solution.py:119
  481.2 90.0 %collective-permute-start.15 = (f32[512,2048]{1,0:T(8,128)}, f32[512,2048]{1,0:T(8,128)}, u32[]{:S(2)}, u32[]{:S(2)}) collective-permute-start(f32[512,2048]{1,0:T(8,128)} %add_add_fusion.1), channel_id=1, source_target_pairs={{0,4},{4,8},{8,12},{12,0},{1,5},{5,9},{9,13},{13,1},{2,6},{6,10},{... | collective-permute-start | bytes 12582920 | tf_op jit(solution)/shard_map/ppermute | solution.py:139
  481.2 9.8 %copy-start.2 = (f32[1,2048,512]{2,1,0:T(8,128)S(1)}, f32[1,2048,512]{2,1,0:T(8,128)}, u32[]{:S(2)}) copy-start(f32[1,2048,512]{2,1,0:T(8,128)} %param.7) | copy-start | bytes 12582916
  481.2 38.9 %collective-permute-start.18 = (f32[1024,512]{1,0:T(8,128)S(1)}, f32[1024,512]{1,0:T(8,128)S(1)}, u32[]{:S(2)}, u32[]{:S(2)}) collective-permute-start(f32[1024,512]{1,0:T(8,128)S(1)} %get-tuple-element.4), channel_id=1, source_target_pairs={{0,1},{2,3},{4,5},{6,7},{9,8},{11,10},{13,12},{15,14},{16,17},{18,... | collective-permute-start | bytes 6291464 | tf_op jit(solution)/shard_map/ppermute | solution.py:120
  491.0 7.5 %slice-start = ((s8[8388608]{0:T(1024)(128)(4,1)}), s8[4194304]{0:T(1024)(128)(4,1)S(1)}, s32[]{:S(2)}) async-start(s8[8388608]{0:T(1024)(128)(4,1)} %bitcast.28), calls=%async_computation | async-start | bytes 8388608
  493.5 4.9 slice-start.1
  513.9 57.3 %copy-start.3 = (f32[512,2048]{1,0:T(8,128)}, f32[512,2048]{1,0:T(8,128)S(1)}, u32[]{:S(2)}) copy-start(f32[512,2048]{1,0:T(8,128)S(1)} %fusion.2) | copy-start | bytes 12582916
  536.0 35.2 %copy-start.4 = (f32[512,2048]{1,0:T(8,128)}, f32[512,2048]{1,0:T(8,128)S(1)}, u32[]{:S(2)}) copy-start(f32[512,2048]{1,0:T(8,128)S(1)} %fusion) | copy-start | bytes 12582916
  606.3 4.5 collective-permute-start.19
  612.9 1.4 copy-start.5
  614.4 25.3 %collective-permute-start.20 = (f32[512,1,512]{2,0,1:T(8,128)S(1)}, f32[512,1,512]{2,0,1:T(8,128)S(1)}, u32[]{:S(2)}, u32[]{:S(2)}) collective-permute-start(f32[512,1,512]{2,0,1:T(8,128)S(1)} %constant_dynamic-slice_fusion), channel_id=1, source_target_pairs={{0,2},{1,3},{2,0},{3,1},{4,6},{5,7},{6,4},{7,5},{8,10},{9,11},{10,... | collective-permute-start | bytes 3145736 | tf_op jit(solution)/shard_map/ppermute | solution.py:154
  615.9 23.7 %copy-start.6 = (f32[512,2,512]{2,0,1:T(8,128)S(1)}, f32[512,2,512]{2,0,1:T(8,128)}, u32[]{:S(2)}) copy-start(f32[512,2,512]{2,0,1:T(8,128)} %copy-done.5) | copy-start | bytes 6291460
  615.9 23.7 %copy-start.7 = (f32[1,512,512]{2,1,0:T(8,128)S(1)}, f32[1,512,512]{2,1,0:T(8,128)}, u32[]{:S(2)}) copy-start(f32[1,512,512]{2,1,0:T(8,128)} %param.8) | copy-start | bytes 3145732
